TPU v7x, 32 devices: a whole 2x2x4 slice. The times are simulated.
32 devices in a mesh: group: 2 (over y), sec: 4 (over z), sub: 4 (over x, core).
Axes of the slice: x: 2, y: 2, z: 4, core: 2. Of those that a mesh axis runs over, the one named last changes fastest.
Arguments:
- tokens: bfloat16 [768, 2048], P(('group', 'sec'), 'sub'), parts along dimension 0, may hold values from -6 to 6
- routes: int32 [768, 2], P(('group', 'sec')), parts along dimension 0, may hold values from 0 to 3, all different within a row; in each aligned block of 96 rows (0 to 95, 96 to 191, ...) at most 96 rows name the same one
- router_weight: bfloat16 [2048, 4], replicated, may hold values from -0.25 to 0.25
- gate_weight: bfloat16 [4, 2048, 1536], P('sec', None, 'sub'), may hold values from -0.125 to 0.125
- up_weight: bfloat16 [4, 2048, 1536], P('sec', None, 'sub'), may hold values from -0.125 to 0.125
- down_weight: bfloat16 [4, 1536, 2048], P('sec', 'sub'), may hold values from -0.15625 to 0.15625
Outputs:
- mixed: bfloat16 [768, 2048], P(('group', 'sec'), 'sub'), parts along dimension 0
There are 2 independent parts, one for each index of `group`. A program takes and returns all parts, laid end to end along the dimension named above; an argument that names none is the same for every part. Nothing has to cross between parts.
Inputs may be any that keep to these rules, and one draw needn't show every extreme that they name: `routes`: A row names 2 different experts. In each aligned block of 96 rows no expert is named more than 96 times, a bound that some block reaches.
All inputs are finite; a program needn't handle non-finite values.
Results may differ from a plain program's by a relative error of at most 0.012.
Values may be sent and summed in bfloat16 or wider, within the bound.
A program may use at most 64 MiB of HBM per device.

v0:
```python
import jax
import jax.numpy as jnp
from jax import lax
from jax.sharding import PartitionSpec as P


def local(tokens, routes, router_weight, gate_weight, up_weight, down_weight):
    rows, top = routes.shape
    experts = router_weight.shape[1]
    slots = 2 * rows * top // experts
    flat_ids = routes.reshape(-1)
    onehot = (flat_ids[:, None] == jnp.arange(experts, dtype=jnp.int32)[None, :]).astype(jnp.int32)
    before = jnp.cumsum(onehot, axis=0) - onehot
    position = jnp.sum(before * onehot, axis=1)
    target = flat_ids * slots + position
    placing = target[None, :] == jnp.arange(experts * slots, dtype=jnp.int32)[:, None]
    dispatch = jnp.sum(
        placing.reshape(experts * slots, rows, top).astype(jnp.int32), axis=2
    ).astype(jnp.bfloat16)
    full_rows = lax.all_gather(tokens, "sub", axis=1, tiled=True)
    logits = jnp.dot(full_rows, router_weight, preferred_element_type=jnp.float32)
    outgoing = jnp.dot(dispatch, full_rows, preferred_element_type=jnp.float32).astype(jnp.bfloat16)
    arrived = lax.all_to_all(
        outgoing.reshape(experts, slots, -1), "sec", split_axis=0, concat_axis=0, tiled=True
    )
    arrived = arrived.reshape(experts * slots, -1)
    chosen = jnp.sum(
        onehot.reshape(rows, top, experts).astype(jnp.float32) * logits[:, None, :], axis=2
    )
    raised = jnp.exp(chosen)
    gates = (raised / jnp.sum(raised, axis=1, keepdims=True)).astype(jnp.bfloat16)
    weighted = jnp.where(placing, gates.reshape(-1)[None, :], jnp.zeros((), jnp.bfloat16))
    combine = jnp.sum(
        weighted.reshape(experts * slots, rows, top).astype(jnp.float32), axis=2
    ).astype(jnp.bfloat16)
    gate_part = jnp.dot(arrived, gate_weight[0], preferred_element_type=jnp.float32)
    up_part = jnp.dot(arrived, up_weight[0], preferred_element_type=jnp.float32)
    hidden = (jax.nn.silu(gate_part) * up_part).astype(jnp.bfloat16)
    partial_value = jnp.dot(hidden, down_weight[0], preferred_element_type=jnp.float32).astype(
        jnp.bfloat16
    )
    contract = (((0,), (0,)), ((), ()))
    returned = lax.all_to_all(
        partial_value.reshape(experts, slots, -1), "sec", split_axis=0, concat_axis=0, tiled=True
    )
    returned = returned.reshape(experts * slots, -1)
    combined = lax.dot_general(combine, returned, contract, preferred_element_type=jnp.float32)
    mixed = lax.psum_scatter(combined.astype(jnp.bfloat16), "sub", scatter_dimension=1, tiled=True)
    return mixed


def solution(mesh):
    placed = (
        P(("group", "sec"), "sub"),
        P(("group", "sec"), None),
        P(),
        P("sec", None, "sub"),
        P("sec", None, "sub"),
        P("sec", "sub", None),
    )
    return jax.shard_map(
        local, mesh=mesh, in_specs=placed, out_specs=P(("group", "sec"), "sub"), check_vma=False
    )
```

profile of v0, /device:TPU:0, one launch (start us, length us, event | category | flops | bytes accessed | tf_op | source)
XLA Modules:
  0.0 136.2 jit_solution(10902128622082048796)
XLA Ops:
  6.5 0.9 copy.25
  7.4 0.1 eq.44
  7.6 1.2 reduce-window.6
  8.8 0.1 slice.12
  8.9 0.1 copy.26
  9.1 0.1 copy.27
  9.2 0.1 add_bitcast_fusion
  9.3 0.1 reduce_sum.51
  9.4 0.1 copy.28
  9.5 0.7 multiply_add_fusion
  10.2 0.1 convert_reduce_fusion
  10.3 0.5 copy-done.2
  10.7 8.1 %all_gather.3 = bf16[96,2048]{1,0:T(8,128)(2,1)S(1)} all-gather(bf16[96,512]{1,0:T(8,128)(2,1)} %param.6), channel_id=1, replica_groups=mesh['group'=2,'sec'=4,'sub'=4] {'sub'}, dimensions={1}, use_global_device_ids=true | all-gather | bytes 491520 | tf_op jit(solution)/shard_map/all_gather | solution.py:20
  18.8 0.6 convolution_convert_fusion.1
  19.4 42.3 %all_to_all.10 = bf16[4,96,2048]{2,1,0:T(8,128)(2,1)S(1)} all-to-all(bf16[4,96,2048]{2,1,0:T(8,128)(2,1)S(1)} %bitcast.35), channel_id=1, replica_groups=mesh['group'=2,'sec'=4,'sub'=4] {'sec'}, dimensions={0} | all-to-all | bytes 3145728 | tf_op jit(solution)/shard_map/all_to_all | solution.py:23
  61.7 1.8 %fusion.3 = f32[384,384]{1,0:T(8,128)} fusion(bf16[384,2048]{1,0:T(8,128)(2,1)S(1)} %bitcast.38, bf16[1,2048,384]{2,1,0:T(8,128)(2,1)S(1)} %copy-done.3), kind=kOutput, calls=%fused_computation.6 | convolution fusion | flops 603979776 | bytes 3735552 | tf_op jit(solution)/shard_map/dot_general | solution.py:36
  63.5 4.5 %convolution_convert_fusion = bf16[384,2048]{1,0:T(8,128)(2,1)} fusion(bf16[1,384,2048]{2,1,0:T(8,128)(2,1)S(1)} %copy-done, bf16[384,2048]{1,0:T(8,128)(2,1)S(1)} %bitcast.39, bf16[1,2048,384]{2,1,0:T(8,128)(2,1)} %param.10, f32[384,384]{1,0:T(8,128)} %fusion.3), kind=kOutput, calls=%fused_computation | convolution fusion | flops 1209630720 | bytes 6881280 | tf_op jit(solution)/shard_map/dot_general | solution.py:39
  68.1 3.7 %all-to-all-start.1 = ((bf16[4,96,2048]{2,1,0:T(8,128)(2,1)}), bf16[4,96,2048]{2,1,0:T(8,128)(2,1)S(1)}, u32[]{:S(2)}, u32[]{:S(2)}) async-start(bf16[4,96,2048]{2,1,0:T(8,128)(2,1)} %bitcast.37), calls=%async_computation.1 | async-start | bytes 3145728 | tf_op jit(solution)/shard_map/all_to_all | solution.py:43
  71.8 0.2 fusion.25
  72.0 0.7 multiply_reduce_fusion
  72.8 0.8 fusion.20
  73.6 34.8 %all-to-all-done.1 = bf16[4,96,2048]{2,1,0:T(8,128)(2,1)S(1)} async-done(((bf16[4,96,2048]{2,1,0:T(8,128)(2,1)}), bf16[4,96,2048]{2,1,0:T(8,128)(2,1)S(1)}, u32[]{:S(2)}, u32[]{:S(2)}) %all-to-all-start.1) | async-done | bytes 1572896 | tf_op jit(solution)/shard_map/all_to_all | solution.py:43
  108.4 1.2 convolution_convert_fusion.2
  109.6 19.8 %reduce-scatter.2.cloned.1.call-done = bf16[96,512]{1,0:T(8,128)(2,1)} async-done(((bf16[96,2048]{1,0:T(8,128)(2,1)}), bf16[96,512]{1,0:T(8,128)(2,1)}) %reduce-scatter.2.cloned.1.call-update) | async-done | bytes 98320 | tf_op jit(solution)/shard_map/reduce_scatter | solution.py:48
  (18 shorter events, 0.2 us)
Async XLA Ops:
  6.5 57.0 %copy-start = (bf16[1,384,2048]{2,1,0:T(8,128)(2,1)S(1)}, bf16[1,384,2048]{2,1,0:T(8,128)(2,1)}, u32[]{:S(2)}) copy-start(bf16[1,384,2048]{2,1,0:T(8,128)(2,1)} %param.11) | copy-start | bytes 4718596
  10.2 0.6 copy-start.2
  19.4 42.3 %copy-start.3 = (bf16[1,2048,384]{2,1,0:T(8,128)(2,1)S(1)}, bf16[1,2048,384]{2,1,0:T(8,128)(2,1)}, u32[]{:S(2)}) copy-start(bf16[1,2048,384]{2,1,0:T(8,128)(2,1)} %param.9) | copy-start | bytes 4718596
  68.1 3.8 %copy-start.1 = (bf16[2048,4]{0,1:T(4,128)(2,1)S(1)}, bf16[2048,4]{0,1:T(4,128)(2,1)}, u32[]{:S(2)}) copy-start(bf16[2048,4]{0,1:T(4,128)(2,1)} %param.8) | copy-start | bytes 49156
  68.1 40.3 %all-to-all-start.1 = ((bf16[4,96,2048]{2,1,0:T(8,128)(2,1)}), bf16[4,96,2048]{2,1,0:T(8,128)(2,1)S(1)}, u32[]{:S(2)}, u32[]{:S(2)}) async-start(bf16[4,96,2048]{2,1,0:T(8,128)(2,1)} %bitcast.37), calls=%async_computation.1 | async-start | bytes 3145728 | tf_op jit(solution)/shard_map/all_to_all | solution.py:43
  71.8 57.6 %reduce-scatter.2.cloned.1.call-start = ((), (), s32[]{:S(2)}) async-start(), calls=%async_computation.3 | async-start | bytes 491520 | tf_op jit(solution)/shard_map/reduce_scatter | solution.py:48
Sparse Core Ops, SparseCore 0:
  109.7 19.5 reduce-scatter.1
where the time goes:
time: 137 us; the launch traced here: 136 us
  waiting for transfers between devices  54.5 us (40%)
  blocking collectives  50.4 us (37%)
  between operations  13.5 us (10%)
  matrix products  8.3 us (6%)
  starting transfers between devices  3.73 us (3%)
  other arithmetic  3.72 us (3%)
  local copies, waits for them, and re-layouts  2.01 us (1%)
    all_to_all x1, blocking collectives, local(): lax.all_to_all(outgoing.reshape(experts, slots, -1), 'sec', split_axis=0,...  42.3 us
    all_to_all x1, waiting for transfers between devices, local(): lax.all_to_all(partial_value.reshape(experts, slots, -1), 'sec', split_ax...  34.8 us
    reduce_scatter x1, waiting for transfers between devices, local(): lax.psum_scatter(combined.astype(jnp.bfloat16), 'sub', scatter_dimension=...  19.8 us
    all_gather x1, blocking collectives, local(): full_rows = lax.all_gather(tokens, 'sub', axis=1, tiled=True)  8.1 us
    dot_general x1, matrix products, local(): jnp.dot(hidden, down_weight[0], preferred_element_type=jnp.float32)  4.54 us
    all_to_all x1, starting transfers between devices, local(): lax.all_to_all(partial_value.reshape(experts, slots, -1), 'sec', split_ax...  3.69 us
  transfers between devices with their start and end apart: 2, of which 2 were waited for; matrix products, arithmetic and copies ran while one was open for 1% of the time, Pallas kernels for 0%

commit v1 on v0

--- a/solution.py
+++ b/solution.py
@@ -1,10 +1,12 @@
 import jax
 import jax.numpy as jnp
 from jax import lax
+from jax.experimental import pallas as pl
+from jax.experimental.pallas import tpu as pltpu
 from jax.sharding import PartitionSpec as P
 
 
-def local(tokens, routes, router_weight, gate_weight, up_weight, down_weight):
+def routed(tokens, routes, router_weight, gate_weight, up_weight, down_weight):
     rows, top = routes.shape
     experts = router_weight.shape[1]
     slots = 2 * rows * top // experts
@@ -49,7 +51,226 @@
     return mixed
 
 
+def flip(index, step):
+    if step == 0:
+        return index
+    if step == 1:
+        return index + 1 - 2 * (index % 2)
+    if step == 2:
+        return (index + 2) % 4
+    return 3 - index
+
+
+def kernel(
+    tokens, routes, router, gate_w, up_w, down_w, out,
+    x, wide, down, keep, core_out, core_in, side_out, side_in, far_out, far_in,
+    load_sem, send_sem, recv_sem,
+):
+    group, sec, sub = (lax.axis_index(name) for name in ("group", "sec", "sub"))
+    width = tokens.shape[1]
+    hidden_units = gate_w.shape[2]
+    rows, top = tokens.shape[0], routes.shape[0]
+
+    loads = [pltpu.make_async_copy(tokens, x.at[0, 0], load_sem.at[0])]
+    for j in range(4):
+        part = pl.ds(pl.multiple_of(flip(sub, j) * width, width), width)
+        loads.append(
+            pltpu.make_async_copy(
+                gate_w.at[0, part, :], wide.at[j, :, pl.ds(0, hidden_units)], load_sem.at[1 + j]
+            )
+        )
+        loads.append(
+            pltpu.make_async_copy(
+                up_w.at[0, part, :], wide.at[j, :, pl.ds(hidden_units, hidden_units)],
+                load_sem.at[5 + j],
+            )
+        )
+    for j in range(4):
+        part = pl.ds(pl.multiple_of(flip(sub, j) * width, width), width)
+        loads.append(pltpu.make_async_copy(down_w.at[0, :, part], down.at[j], load_sem.at[9 + j]))
+    for load in loads:
+        load.start()
+
+    barrier = pltpu.get_barrier_semaphore()
+    partners = [(group, flip(sec, k), sub) for k in (1, 2, 3)]
+    partners += [(group, sec, flip(sub, j)) for j in (1, 2)]
+    for partner in partners:
+        pl.semaphore_signal(
+            barrier, inc=1, device_id=partner, device_id_type=pl.DeviceIdType.MESH
+        )
+    pl.semaphore_wait(barrier, len(partners))
+
+    def copy(source, target, number, over_sec, over_sub):
+        return pltpu.make_async_remote_copy(
+            src_ref=source,
+            dst_ref=target,
+            send_sem=send_sem.at[number],
+            recv_sem=recv_sem.at[number],
+            device_id=(group, flip(sec, over_sec), flip(sub, over_sub)),
+            device_id_type=pl.DeviceIdType.MESH,
+        )
+
+    gather_far = [None] + [copy(x.at[0, 0], x.at[k, 0], k, k, 0) for k in (1, 2, 3)]
+    gather_core = [copy(x.at[k, 0], x.at[k, 1], 4 + k, 0, 1) for k in range(4)]
+    gather_side = [copy(x.at[k, 0], x.at[k, 2], 8 + k, 0, 2) for k in range(4)]
+    gather_last = [copy(x.at[k, 2], x.at[k, 3], 12 + k, 0, 1) for k in range(4)]
+    sum_core = [copy(core_out.at[k], core_in.at[k], 16 + k, 0, 1) for k in range(4)]
+    sum_side = [copy(side_out.at[k], side_in.at[k], 20 + k, 0, 2) for k in range(4)]
+    sum_far = [None] + [copy(far_out.at[k], far_in.at[k], 24 + k, k, 0) for k in (1, 2, 3)]
+
+    loads[0].wait()
+    gather_side[0].start()
+    for k in (1, 2, 3):
+        gather_far[k].start()
+    gather_core[0].start()
+
+    def pass_on(k):
+        gather_far[k].wait_recv()
+        gather_side[k].start()
+        gather_core[k].start()
+
+    def pass_last(k):
+        gather_side[k].wait_recv()
+        gather_last[k].start()
+
+    def expert(k):
+        gather_core[k].wait_recv()
+        gather_last[k].wait_recv()
+        both = jnp.dot(x[k, 0], wide[0], preferred_element_type=jnp.float32)
+        for j in (1, 2, 3):
+            both += jnp.dot(x[k, j], wide[j], preferred_element_type=jnp.float32)
+        hidden = (jax.nn.silu(both[:, :hidden_units]) * both[:, hidden_units:]).astype(jnp.bfloat16)
+        if k == 0:
+            for load in loads[9:]:
+                load.wait()
+        for place, j in enumerate((1, 3)):
+            core_out[k, place] = jnp.dot(
+                hidden, down[j], preferred_element_type=jnp.float32
+            ).astype(jnp.bfloat16)
+        sum_core[k].start()
+        for place, j in enumerate((0, 2)):
+            keep[k, place] = jnp.dot(hidden, down[j], preferred_element_type=jnp.float32)
+
+    def to_side(k):
+        sum_core[k].wait_recv()
+        side_out[k] = (keep[k, 1] + core_in[k, 1].astype(jnp.float32)).astype(jnp.bfloat16)
+        sum_side[k].start()
+        keep[k, 0] = keep[k, 0] + core_in[k, 0].astype(jnp.float32)
+
+    def to_far(k):
+        sum_side[k].wait_recv()
+        total = keep[k, 0] + side_in[k].astype(jnp.float32)
+        if k == 0:
+            keep[k, 0] = total
+        else:
+            far_out[k] = total.astype(jnp.bfloat16)
+            sum_far[k].start()
+
+    def gates():
+        logits = jnp.zeros((router.shape[0], rows), jnp.float32)
+        for j in range(4):
+            part = pl.ds(pl.multiple_of(flip(sub, j) * width, width), width)
+            logits += lax.dot_general(
+                router[:, part], x[0, j], (((1,), (1,)), ((), ())),
+                preferred_element_type=jnp.float32,
+            )
+        names = [routes[t : t + 1, :] for t in range(top)]
+        raised = []
+        for t in range(top):
+            chosen = jnp.zeros((1, rows), jnp.float32)
+            for e in range(router.shape[0]):
+                chosen = jnp.where(names[t] == e, logits[e : e + 1, :], chosen)
+            raised.append(jnp.exp(chosen))
+        whole = sum(raised)
+        shares = [(r / whole).astype(jnp.bfloat16).astype(jnp.float32) for r in raised]
+        lines = []
+        for k in range(4):
+            line = jnp.zeros((1, rows), jnp.float32)
+            for t in range(top):
+                line += jnp.where(names[t] == flip(sec, k), shares[t], 0.0)
+            lines.append(line)
+        lines.append(jnp.zeros((4, rows), jnp.float32))
+        return jnp.transpose(jnp.concatenate(lines, axis=0))
+
+    pass_last(0)
+    pass_on(1)
+    for load in loads[1:9]:
+        load.wait()
+    expert(0)
+    pass_last(1)
+    pass_on(2)
+    to_side(0)
+    expert(1)
+    pass_last(2)
+    pass_on(3)
+    to_side(1)
+    to_far(0)
+    expert(2)
+    pass_last(3)
+    to_side(2)
+    to_far(1)
+    expert(3)
+    to_far(2)
+    weights = gates()
+    to_side(3)
+    mixed = weights[:, 0:1] * keep[0, 0]
+    to_far(3)
+    for k in (1, 2, 3):
+        sum_far[k].wait_recv()
+        mixed += weights[:, k : k + 1] * far_in[k].astype(jnp.float32)
+    out[...] = mixed.astype(jnp.bfloat16)
+    for k in range(4):
+        gather_core[k].wait_send()
+        gather_side[k].wait_send()
+        gather_last[k].wait_send()
+        sum_core[k].wait_send()
+        sum_side[k].wait_send()
+        if k > 0:
+            gather_far[k].wait_send()
+            sum_far[k].wait_send()
+
+
+def dense(tokens, routes, router_weight, gate_weight, up_weight, down_weight):
+    rows, width = tokens.shape
+    hidden_units = gate_weight.shape[2]
+    hbm, vmem = pl.BlockSpec(memory_space=pl.ANY), pl.BlockSpec(memory_space=pltpu.VMEM)
+    block = (rows, width)
+    return pl.pallas_call(
+        kernel,
+        out_shape=jax.ShapeDtypeStruct(block, jnp.bfloat16),
+        in_specs=[hbm, vmem, vmem, hbm, hbm, hbm],
+        out_specs=vmem,
+        scratch_shapes=[
+            pltpu.VMEM((4, 4) + block, jnp.bfloat16),
+            pltpu.VMEM((4, width, 2 * hidden_units), jnp.bfloat16),
+            pltpu.VMEM((4, hidden_units, width), jnp.bfloat16),
+            pltpu.VMEM((4, 2) + block, jnp.float32),
+            pltpu.VMEM((4, 2) + block, jnp.bfloat16),
+            pltpu.VMEM((4, 2) + block, jnp.bfloat16),
+            pltpu.VMEM((4,) + block, jnp.bfloat16),
+            pltpu.VMEM((4,) + block, jnp.bfloat16),
+            pltpu.VMEM((4,) + block, jnp.bfloat16),
+            pltpu.VMEM((4,) + block, jnp.bfloat16),
+            pltpu.SemaphoreType.DMA((13,)),
+            pltpu.SemaphoreType.DMA((28,)),
+            pltpu.SemaphoreType.DMA((28,)),
+        ],
+        compiler_params=pltpu.CompilerParams(
+            collective_id=0, has_side_effects=True, vmem_limit_bytes=40 * 2**20
+        ),
+    )(tokens, routes.T, router_weight.T, gate_weight, up_weight, down_weight)
+
+
 def solution(mesh):
+    def local(*args):
+        tokens, routes, router_weight = args[:3]
+        rows, top = routes.shape
+        experts = router_weight.shape[1]
+        sec, sub = mesh.shape["sec"], mesh.shape["sub"]
+        if experts == sec == sub == 4 and 2 * rows * top // experts >= rows and rows % 16 == 0:
+            return dense(*args)
+        return routed(*args)
+
     placed = (
         P(("group", "sec"), "sub"),
         P(("group", "sec"), None),

time: 137 us -> 44.4 us (0.32)
  waiting for transfers between devices: 54.5 us -> 0 us
  blocking collectives: 50.4 us -> 0 us
  Pallas kernels: 0 us -> 36.9 us
  between operations: 13.5 us -> 0.02 us
  matrix products: 8.3 us -> 0 us
  local copies, waits for them, and re-layouts: 2.01 us -> 7.15 us
  starting transfers between devices: 3.73 us -> 0 us
  other arithmetic: 3.72 us -> 0 us
    all_to_all x1 -> x0, blocking collectives: 42.3 us -> none  [local(): lax.all_to_all(outgoing.reshape(experts, slots, -1), 'sec', split_axis=0,...]
    pallas_call x0 -> x1, Pallas kernels: none -> 36.9 us  [dense(): pl.pallas_call(kernel, out_shape=jax.ShapeDtypeStruct(block, jnp.bfloat16...]
    all_to_all x1 -> x0, waiting for transfers between devices: 34.8 us -> none  [local(): lax.all_to_all(partial_value.reshape(experts, slots, -1), 'sec', split_ax...]
    reduce_scatter x1 -> x0, waiting for transfers between devices: 19.8 us -> none  [local(): lax.psum_scatter(combined.astype(jnp.bfloat16), 'sub', scatter_dimension=...]
    dot_general x5 -> x0, matrix products: 8.3 us -> none  [the longest x1 4.54 us: local(): jnp.dot(hidden, down_weight[0], preferred_element_type=jnp.float32)]
    all_gather x1 -> x0, blocking collectives: 8.1 us -> none  [local(): full_rows = lax.all_gather(tokens, 'sub', axis=1, tiled=True)]
    unnamed x10 -> x13, local copies, waits for them, and re-layouts: 1.38 us -> 7.15 us
    all_to_all x1 -> x0, starting transfers between devices: 3.69 us -> none  [local(): lax.all_to_all(partial_value.reshape(experts, slots, -1), 'sec', split_ax...]
  transfers between devices with their start and end apart: 2 -> 0, of which waited for: 2 -> 0; matrix products, arithmetic and copies ran while one was open for 1% -> 0% of each run, Pallas kernels for 0% -> 0%
where the time goes in v1:
time: 44.4 us; the launch traced here: 44.1 us
  Pallas kernels  36.9 us (83%)
  local copies, waits for them, and re-layouts  7.15 us (16%)
    pallas_call x1, Pallas kernels, dense(): pl.pallas_call(kernel, out_shape=jax.ShapeDtypeStruct(block, jnp.bfloat16...  36.9 us
    unnamed x13, local copies, waits for them, and re-layouts  7.15 us

profile of v1, /device:TPU:0, one launch (start us, length us, event | category | flops | bytes accessed | tf_op | source)
XLA Modules:
  0.0 44.1 jit_solution(13017703262288941953)
XLA Ops:
  0.0 0.0 copy-start
  0.0 1.4 %copy-done = bf16[1,2048,384]{2,1,0:T(8,128)(2,1)S(1)} copy-done((bf16[1,2048,384]{2,1,0:T(8,128)(2,1)S(1)}, bf16[1,2048,384]{2,1,0:T(8,128)(2,1)}, u32[]{:S(2)}) %copy-start) | copy-done | bytes 1572888
  1.4 0.0 copy-start.1
  1.4 1.4 %copy-done.1 = bf16[1,2048,384]{2,1,0:T(8,128)(2,1)S(1)} copy-done((bf16[1,2048,384]{2,1,0:T(8,128)(2,1)S(1)}, bf16[1,2048,384]{2,1,0:T(8,128)(2,1)}, u32[]{:S(2)}) %copy-start.1) | copy-done | bytes 1572888
  2.8 0.0 copy-start.2
  2.8 1.4 %copy-done.2 = bf16[1,384,2048]{2,1,0:T(8,128)(2,1)S(1)} copy-done((bf16[1,384,2048]{2,1,0:T(8,128)(2,1)S(1)}, bf16[1,384,2048]{2,1,0:T(8,128)(2,1)}, u32[]{:S(2)}) %copy-start.2) | copy-done | bytes 1572888
  4.2 0.0 copy-start.3
  4.2 0.9 %copy-done.3 = bf16[96,512]{1,0:T(8,128)(2,1)S(1)} copy-done((bf16[96,512]{1,0:T(8,128)(2,1)S(1)}, bf16[96,512]{1,0:T(8,128)(2,1)}, u32[]{:S(2)}) %copy-start.3) | copy-done | bytes 98328
  5.1 0.0 copy-start.4
  5.1 0.7 %copy-done.4 = bf16[2048,4]{0,1:T(4,128)(2,1)S(1)} copy-done((bf16[2048,4]{0,1:T(4,128)(2,1)S(1)}, bf16[2048,4]{0,1:T(4,128)(2,1)}, u32[]{:S(2)}) %copy-start.4) | copy-done | bytes 16408
  5.8 0.0 copy-start.5
  5.8 0.7 %copy-done.5 = s32[96,2]{0,1:T(2,128)S(1)} copy-done((s32[96,2]{0,1:T(2,128)S(1)}, s32[96,2]{0,1:T(2,128)}, u32[]{:S(2)}) %copy-start.5) | copy-done | bytes 792
  6.5 36.9 %shard_map.64 = bf16[96,512]{1,0:T(8,128)(2,1)S(1)} custom-call(bf16[96,512]{1,0:T(8,128)(2,1)S(1)} %copy-done.3, s32[2,96]{1,0:T(2,128)S(1)} %bitcast.3, bf16[4,2048]{1,0:T(4,128)(2,1)S(1)} %bitcast.2, bf16[1,2048,384]{2,1,0:T(8,128)(2,1)S(1)} %copy-done, bf16[1,2048,384]{2,1,0:T(8,128)(2,1)S(1)} %copy-done.1, bf16[1,384,2048]{2,1,0:T(8,128)(2,1)S(1)} %copy-done.2), custom_call_target="tpu_custom_call" | custom-call | tf_op jit(solution)/shard_map/pallas_call | solution.py:238
  43.5 0.6 %copy.8 = bf16[96,512]{1,0:T(8,128)(2,1)} copy(bf16[96,512]{1,0:T(8,128)(2,1)S(1)} %shard_map.64) | data formatting | bytes 196608
Async XLA Ops:
  0.0 1.4 %copy-start = (bf16[1,2048,384]{2,1,0:T(8,128)(2,1)S(1)}, bf16[1,2048,384]{2,1,0:T(8,128)(2,1)}, u32[]{:S(2)}) copy-start(bf16[1,2048,384]{2,1,0:T(8,128)(2,1)} %gate_w.1) | copy-start | bytes 4718596
  1.4 1.4 %copy-start.1 = (bf16[1,2048,384]{2,1,0:T(8,128)(2,1)S(1)}, bf16[1,2048,384]{2,1,0:T(8,128)(2,1)}, u32[]{:S(2)}) copy-start(bf16[1,2048,384]{2,1,0:T(8,128)(2,1)} %up_w.1) | copy-start | bytes 4718596
  2.8 1.4 %copy-start.2 = (bf16[1,384,2048]{2,1,0:T(8,128)(2,1)S(1)}, bf16[1,384,2048]{2,1,0:T(8,128)(2,1)}, u32[]{:S(2)}) copy-start(bf16[1,384,2048]{2,1,0:T(8,128)(2,1)} %down_w.1) | copy-start | bytes 4718596
  4.2 0.9 %copy-start.3 = (bf16[96,512]{1,0:T(8,128)(2,1)S(1)}, bf16[96,512]{1,0:T(8,128)(2,1)}, u32[]{:S(2)}) copy-start(bf16[96,512]{1,0:T(8,128)(2,1)} %tokens.1) | copy-start | bytes 294916
  5.1 0.7 %copy-start.4 = (bf16[2048,4]{0,1:T(4,128)(2,1)S(1)}, bf16[2048,4]{0,1:T(4,128)(2,1)}, u32[]{:S(2)}) copy-start(bf16[2048,4]{0,1:T(4,128)(2,1)} %param.8) | copy-start | bytes 49156
  5.8 0.7 %copy-start.5 = (s32[96,2]{0,1:T(2,128)S(1)}, s32[96,2]{0,1:T(2,128)}, u32[]{:S(2)}) copy-start(s32[96,2]{0,1:T(2,128)} %param.7) | copy-start | bytes 2308

commit v2 on v1

--- a/solution.py
+++ b/solution.py
@@ -1,3 +1,4 @@
+import functools
 import jax
 import jax.numpy as jnp
 from jax import lax
@@ -51,6 +52,9 @@
     return mixed
 
 
+PIECES = 2
+
+
 def flip(index, step):
     if step == 0:
         return index
@@ -62,14 +66,15 @@
 
 
 def kernel(
-    tokens, routes, router, gate_w, up_w, down_w, out,
-    x, wide, down, keep, core_out, core_in, side_out, side_in, far_out, far_in,
+    tokens, routes_hbm, router_hbm, gate_w, up_w, down_w, out,
+    routes, router, x, wide, down, keep, core_out, core_in, side_out, side_in, far_out, far_in,
     load_sem, send_sem, recv_sem,
 ):
     group, sec, sub = (lax.axis_index(name) for name in ("group", "sec", "sub"))
     width = tokens.shape[1]
     hidden_units = gate_w.shape[2]
     rows, top = tokens.shape[0], routes.shape[0]
+    experts = router.shape[0]
 
     loads = [pltpu.make_async_copy(tokens, x.at[0, 0], load_sem.at[0])]
     for j in range(4):
@@ -88,6 +93,8 @@
     for j in range(4):
         part = pl.ds(pl.multiple_of(flip(sub, j) * width, width), width)
         loads.append(pltpu.make_async_copy(down_w.at[0, :, part], down.at[j], load_sem.at[9 + j]))
+    loads.append(pltpu.make_async_copy(routes_hbm, routes, load_sem.at[13]))
+    loads.append(pltpu.make_async_copy(router_hbm, router, load_sem.at[14]))
     for load in loads:
         load.start()
 
@@ -100,7 +107,11 @@
         )
     pl.semaphore_wait(barrier, len(partners))
 
-    def copy(source, target, number, over_sec, over_sub):
+    used = [0]
+
+    def copy(source, target, over_sec, over_sub):
+        number = used[0]
+        used[0] += 1
         return pltpu.make_async_remote_copy(
             src_ref=source,
             dst_ref=target,
@@ -110,38 +121,42 @@
             device_id_type=pl.DeviceIdType.MESH,
         )
 
-    gather_far = [None] + [copy(x.at[0, 0], x.at[k, 0], k, k, 0) for k in (1, 2, 3)]
-    gather_core = [copy(x.at[k, 0], x.at[k, 1], 4 + k, 0, 1) for k in range(4)]
-    gather_side = [copy(x.at[k, 0], x.at[k, 2], 8 + k, 0, 2) for k in range(4)]
-    gather_last = [copy(x.at[k, 2], x.at[k, 3], 12 + k, 0, 1) for k in range(4)]
-    sum_core = [copy(core_out.at[k], core_in.at[k], 16 + k, 0, 1) for k in range(4)]
-    sum_side = [copy(side_out.at[k], side_in.at[k], 20 + k, 0, 2) for k in range(4)]
-    sum_far = [None] + [copy(far_out.at[k], far_in.at[k], 24 + k, k, 0) for k in (1, 2, 3)]
-
-    loads[0].wait()
-    gather_side[0].start()
-    for k in (1, 2, 3):
-        gather_far[k].start()
-    gather_core[0].start()
-
-    def pass_on(k):
-        gather_far[k].wait_recv()
-        gather_side[k].start()
-        gather_core[k].start()
-
-    def pass_last(k):
-        gather_side[k].wait_recv()
-        gather_last[k].start()
+    cuts = [pl.ds(h * (rows // PIECES), rows // PIECES) for h in range(PIECES)]
+
+    def copies(source, target, over_sec, over_sub):
+        return [copy(source.at[cut], target.at[cut], over_sec, over_sub) for cut in cuts]
+
+    gather_far = {k: copies(x.at[0, 0], x.at[k, 0], k, 0) for k in (1, 2, 3)}
+    gather_far["twin"] = copies(x.at[0, 2], x.at[1, 2], 1, 0)
+    gather_core = {k: copies(x.at[k, 0], x.at[k, 1], 0, 1) for k in range(4)}
+    gather_side = {k: copies(x.at[k, 0], x.at[k, 2], 0, 2) for k in (0, 2, 3)}
+    gather_last = {k: copies(x.at[k, 2], x.at[k, 3], 0, 1) for k in range(4)}
+    sum_core = {k: copy(core_out.at[k], core_in.at[k], 0, 1) for k in range(4)}
+    sum_side = {k: copies(side_out.at[k], side_in.at[k], 0, 2) for k in (0, 2, 3)}
+    sum_far = {k: copies(far_out.at[k], far_in.at[k], k, 0) for k in (1, 2, 3)}
+    sum_far["twin"] = copies(far_out.at[0], far_in.at[0], 1, 0)
+    every = range(PIECES)
+
+    def pass_on(k, h):
+        gather_far[k][h].wait_recv()
+        if k != 1:
+            gather_side[k][h].start()
+        gather_core[k][h].start()
+
+    def pass_last(k, h):
+        (gather_far["twin"] if k == 1 else gather_side[k])[h].wait_recv()
+        gather_last[k][h].start()
 
     def expert(k):
-        gather_core[k].wait_recv()
-        gather_last[k].wait_recv()
+        for h in every:
+            gather_core[k][h].wait_recv()
+            gather_last[k][h].wait_recv()
         both = jnp.dot(x[k, 0], wide[0], preferred_element_type=jnp.float32)
         for j in (1, 2, 3):
             both += jnp.dot(x[k, j], wide[j], preferred_element_type=jnp.float32)
         hidden = (jax.nn.silu(both[:, :hidden_units]) * both[:, hidden_units:]).astype(jnp.bfloat16)
         if k == 0:
-            for load in loads[9:]:
+            for load in loads[9:13]:
                 load.wait()
         for place, j in enumerate((1, 3)):
             core_out[k, place] = jnp.dot(
@@ -153,21 +168,34 @@
 
     def to_side(k):
         sum_core[k].wait_recv()
-        side_out[k] = (keep[k, 1] + core_in[k, 1].astype(jnp.float32)).astype(jnp.bfloat16)
-        sum_side[k].start()
-        keep[k, 0] = keep[k, 0] + core_in[k, 0].astype(jnp.float32)
-
-    def to_far(k):
-        sum_side[k].wait_recv()
-        total = keep[k, 0] + side_in[k].astype(jnp.float32)
-        if k == 0:
-            keep[k, 0] = total
-        else:
-            far_out[k] = total.astype(jnp.bfloat16)
-            sum_far[k].start()
+        for h in every:
+            side_out[k, cuts[h]] = (
+                keep[k, 1, cuts[h]] + core_in[k, 1, cuts[h]].astype(jnp.float32)
+            ).astype(jnp.bfloat16)
+            sum_side[k][h].start()
+
+    def to_far(k, h):
+        sum_side[k][h].wait_recv()
+        far_out[k, cuts[h]] = (
+            keep[k, 0, cuts[h]]
+            + core_in[k, 0, cuts[h]].astype(jnp.float32)
+            + side_in[k, cuts[h]].astype(jnp.float32)
+        ).astype(jnp.bfloat16)
+        sum_far[k][h].start()
+
+    def both_to_next():
+        sum_core[1].wait_recv()
+        for place, slot, name in ((1, 0, "twin"), (0, 1, 1)):
+            for h in every:
+                far_out[slot, cuts[h]] = (
+                    keep[1, place, cuts[h]] + core_in[1, place, cuts[h]].astype(jnp.float32)
+                ).astype(jnp.bfloat16)
+                sum_far[name][h].start()
 
     def gates():
-        logits = jnp.zeros((router.shape[0], rows), jnp.float32)
+        loads[13].wait()
+        loads[14].wait()
+        logits = jnp.zeros((experts, rows), jnp.float32)
         for j in range(4):
             part = pl.ds(pl.multiple_of(flip(sub, j) * width, width), width)
             logits += lax.dot_general(
@@ -178,7 +206,7 @@
         raised = []
         for t in range(top):
             chosen = jnp.zeros((1, rows), jnp.float32)
-            for e in range(router.shape[0]):
+            for e in range(experts):
                 chosen = jnp.where(names[t] == e, logits[e : e + 1, :], chosen)
             raised.append(jnp.exp(chosen))
         whole = sum(raised)
@@ -192,55 +220,93 @@
         lines.append(jnp.zeros((4, rows), jnp.float32))
         return jnp.transpose(jnp.concatenate(lines, axis=0))
 
-    pass_last(0)
-    pass_on(1)
+    loads[0].wait()
+    for h in every:
+        gather_side[0][h].start()
+        gather_far[2][h].start()
+    for h in every:
+        gather_core[0][h].start()
+    for h in every:
+        gather_far[1][h].start()
+    for h in range(PIECES - 1):
+        gather_far[2][h].wait_send()
+        gather_far[3][h].start()
+    for h in every:
+        pass_last(0, h)
+        gather_far["twin"][h].start()
+    for h in every:
+        pass_on(2, h)
+    gather_far[2][PIECES - 1].wait_send()
+    gather_far[3][PIECES - 1].start()
+    for h in every:
+        pass_on(1, h)
     for load in loads[1:9]:
         load.wait()
     expert(0)
-    pass_last(1)
-    pass_on(2)
-    to_side(0)
+    for h in every:
+        pass_on(3, h)
+        pass_last(2, h)
+        pass_last(1, h)
+    expert(2)
     expert(1)
-    pass_last(2)
-    pass_on(3)
-    to_side(1)
-    to_far(0)
-    expert(2)
-    pass_last(3)
     to_side(2)
-    to_far(1)
+    for h in every:
+        pass_last(3, h)
+    both_to_next()
     expert(3)
-    to_far(2)
+    to_side(3)
+    for h in every:
+        to_far(2, h)
     weights = gates()
-    to_side(3)
-    mixed = weights[:, 0:1] * keep[0, 0]
-    to_far(3)
-    for k in (1, 2, 3):
-        sum_far[k].wait_recv()
-        mixed += weights[:, k : k + 1] * far_in[k].astype(jnp.float32)
-    out[...] = mixed.astype(jnp.bfloat16)
+    sum_core[0].wait_recv()
+    first, second = weights[:, 0:1], weights[:, 1:2]
+    for h in every:
+        sum_far["twin"][h].wait_recv()
+    side_out[0] = (
+        first * (keep[0, 1] + core_in[0, 1].astype(jnp.float32))
+        + second * far_in[0].astype(jnp.float32)
+    ).astype(jnp.bfloat16)
+    for h in every:
+        sum_side[0][h].start()
+    for h in every:
+        to_far(3, h)
+    for h in every:
+        sum_far[1][h].wait_recv()
+    mixed = (
+        first * (keep[0, 0] + core_in[0, 0].astype(jnp.float32))
+        + second * far_in[1].astype(jnp.float32)
+    )
+    for h in every:
+        sum_far[2][h].wait_recv()
+    mixed += weights[:, 2:3] * far_in[2].astype(jnp.float32)
+    for h in every:
+        sum_side[0][h].wait_recv()
+    mixed += side_in[0].astype(jnp.float32)
+    for h in every:
+        sum_far[3][h].wait_recv()
+    out[...] = (mixed + weights[:, 3:4] * far_in[3].astype(jnp.float32)).astype(jnp.bfloat16)
+    for family in (gather_far, gather_core, gather_side, gather_last, sum_side, sum_far):
+        for name in family:
+            for h in every:
+                if family is not gather_far or name != 2:
+                    family[name][h].wait_send()
     for k in range(4):
-        gather_core[k].wait_send()
-        gather_side[k].wait_send()
-        gather_last[k].wait_send()
         sum_core[k].wait_send()
-        sum_side[k].wait_send()
-        if k > 0:
-            gather_far[k].wait_send()
-            sum_far[k].wait_send()
 
 
 def dense(tokens, routes, router_weight, gate_weight, up_weight, down_weight):
     rows, width = tokens.shape
     hidden_units = gate_weight.shape[2]
-    hbm, vmem = pl.BlockSpec(memory_space=pl.ANY), pl.BlockSpec(memory_space=pltpu.VMEM)
+    hbm, vmem = pl.BlockSpec(memory_space=pltpu.HBM), pl.BlockSpec(memory_space=pltpu.VMEM)
     block = (rows, width)
     return pl.pallas_call(
         kernel,
         out_shape=jax.ShapeDtypeStruct(block, jnp.bfloat16),
-        in_specs=[hbm, vmem, vmem, hbm, hbm, hbm],
+        in_specs=[hbm] * 6,
         out_specs=vmem,
         scratch_shapes=[
+            pltpu.VMEM(routes.shape[::-1], routes.dtype),
+            pltpu.VMEM(router_weight.shape[::-1], router_weight.dtype),
             pltpu.VMEM((4, 4) + block, jnp.bfloat16),
             pltpu.VMEM((4, width, 2 * hidden_units), jnp.bfloat16),
             pltpu.VMEM((4, hidden_units, width), jnp.bfloat16),
@@ -251,12 +317,12 @@
             pltpu.VMEM((4,) + block, jnp.bfloat16),
             pltpu.VMEM((4,) + block, jnp.bfloat16),
             pltpu.VMEM((4,) + block, jnp.bfloat16),
-            pltpu.SemaphoreType.DMA((13,)),
-            pltpu.SemaphoreType.DMA((28,)),
-            pltpu.SemaphoreType.DMA((28,)),
+            pltpu.SemaphoreType.DMA((15,)),
+            pltpu.SemaphoreType.DMA((22 * PIECES + 4,)),
+            pltpu.SemaphoreType.DMA((22 * PIECES + 4,)),
         ],
         compiler_params=pltpu.CompilerParams(
-            collective_id=0, has_side_effects=True, vmem_limit_bytes=40 * 2**20
+            collective_id=0, has_side_effects=True, vmem_limit_bytes=60 * 2**20
         ),
     )(tokens, routes.T, router_weight.T, gate_weight, up_weight, down_weight)
 

time: 44.4 us -> 35.1 us (0.79)
  local copies, waits for them, and re-layouts: 7.15 us -> 1.54 us
  Pallas kernels: 36.9 us -> 33.4 us
    unnamed x13 -> x1, local copies, waits for them, and re-layouts: 7.15 us -> 1.54 us
    pallas_call x1, Pallas kernels: 36.9 us -> 33.4 us  [dense(): pl.pallas_call(kernel, out_shape=jax.ShapeDtypeStruct(block, jnp.bfloat16...]
where the time goes in v2:
time: 35.1 us; the launch traced here: 35 us
  Pallas kernels  33.4 us (95%)
  local copies, waits for them, and re-layouts  1.54 us (4%)
    pallas_call x1, Pallas kernels, dense(): pl.pallas_call(kernel, out_shape=jax.ShapeDtypeStruct(block, jnp.bfloat16...  33.4 us
    unnamed x1, local copies, waits for them, and re-layouts  1.54 us

profile of v2, /device:TPU:0, one launch (start us, length us, event | category | flops | bytes accessed | tf_op | source)
XLA Modules:
  0.0 35.0 jit_solution(15540427374367292553)
XLA Ops:
  0.0 33.4 %shard_map.64 = bf16[96,512]{1,0:T(8,128)(2,1)} custom-call(bf16[96,512]{1,0:T(8,128)(2,1)} %tokens.1, s32[2,96]{1,0:T(2,128)} %bitcast.3, bf16[4,2048]{1,0:T(4,128)(2,1)} %bitcast.2, bf16[1,2048,384]{2,1,0:T(8,128)(2,1)} %gate_w.1, bf16[1,2048,384]{2,1,0:T(8,128)(2,1)} %up_w.1, bf16[1,384,2048]{2,1,0:T(8,128)(2,1)} %down_w.1), custom_call_target="tpu_custom_call" | custom-call | tf_op jit(solution)/shard_map/pallas_call | solution.py:302
  33.4 1.5 %copy.8 = bf16[96,512]{1,0:T(8,128)(2,1)} copy(bf16[96,512]{1,0:T(8,128)(2,1)} %shard_map.64) | data formatting | bytes 196608

commit v3 on v2

--- a/solution.py
+++ b/solution.py
@@ -109,14 +109,14 @@
 
     used = [0]
 
-    def copy(source, target, over_sec, over_sub):
+    def copy(source, target, over_sec, over_sub, landing=None):
         number = used[0]
         used[0] += 1
         return pltpu.make_async_remote_copy(
             src_ref=source,
             dst_ref=target,
             send_sem=send_sem.at[number],
-            recv_sem=recv_sem.at[number],
+            recv_sem=recv_sem.at[number if landing is None else landing],
             device_id=(group, flip(sec, over_sec), flip(sub, over_sub)),
             device_id_type=pl.DeviceIdType.MESH,
         )
@@ -128,6 +128,10 @@
 
     gather_far = {k: copies(x.at[0, 0], x.at[k, 0], k, 0) for k in (1, 2, 3)}
     gather_far["twin"] = copies(x.at[0, 2], x.at[1, 2], 1, 0)
+    relay = [
+        copy(x.at[2, 0].at[cut], x.at[3, 0].at[cut], 1, 0, 2 * PIECES + h)
+        for h, cut in enumerate(cuts)
+    ]
     gather_core = {k: copies(x.at[k, 0], x.at[k, 1], 0, 1) for k in range(4)}
     gather_side = {k: copies(x.at[k, 0], x.at[k, 2], 0, 2) for k in (0, 2, 3)}
     gather_last = {k: copies(x.at[k, 2], x.at[k, 3], 0, 1) for k in range(4)}
@@ -139,6 +143,12 @@
 
     def pass_on(k, h):
         gather_far[k][h].wait_recv()
+        if k == 2:
+
+            @pl.when(inner)
+            def _():
+                relay[h].start()
+
         if k != 1:
             gather_side[k][h].start()
         gather_core[k][h].start()
@@ -228,16 +238,18 @@
         gather_core[0][h].start()
     for h in every:
         gather_far[1][h].start()
-    for h in range(PIECES - 1):
-        gather_far[2][h].wait_send()
-        gather_far[3][h].start()
+    inner = jnp.logical_or(sec == 1, sec == 2)
+
+    @pl.when(inner)
+    def _():
+        for h in every:
+            gather_far[3][h].start()
+
     for h in every:
         pass_last(0, h)
         gather_far["twin"][h].start()
     for h in every:
         pass_on(2, h)
-    gather_far[2][PIECES - 1].wait_send()
-    gather_far[3][PIECES - 1].start()
     for h in every:
         pass_on(1, h)
     for load in loads[1:9]:
@@ -287,9 +299,17 @@
     out[...] = (mixed + weights[:, 3:4] * far_in[3].astype(jnp.float32)).astype(jnp.bfloat16)
     for family in (gather_far, gather_core, gather_side, gather_last, sum_side, sum_far):
         for name in family:
+            if family is gather_far and name == 3:
+                continue
             for h in every:
-                if family is not gather_far or name != 2:
-                    family[name][h].wait_send()
+                family[name][h].wait_send()
+
+    @pl.when(inner)
+    def _():
+        for h in every:
+            gather_far[3][h].wait_send()
+            relay[h].wait_send()
+
     for k in range(4):
         sum_core[k].wait_send()
 
@@ -318,8 +338,8 @@
             pltpu.VMEM((4,) + block, jnp.bfloat16),
             pltpu.VMEM((4,) + block, jnp.bfloat16),
             pltpu.SemaphoreType.DMA((15,)),
-            pltpu.SemaphoreType.DMA((22 * PIECES + 4,)),
-            pltpu.SemaphoreType.DMA((22 * PIECES + 4,)),
+            pltpu.SemaphoreType.DMA((23 * PIECES + 4,)),
+            pltpu.SemaphoreType.DMA((23 * PIECES + 4,)),
         ],
         compiler_params=pltpu.CompilerParams(
             collective_id=0, has_side_effects=True, vmem_limit_bytes=60 * 2**20

time: 35.1 us -> 34.2 us (0.974)
  Pallas kernels: 33.4 us -> 32.5 us
    pallas_call x1, Pallas kernels: 33.4 us -> 32.5 us  [dense(): pl.pallas_call(kernel, out_shape=jax.ShapeDtypeStruct(block, jnp.bfloat16...]
where the time goes in v3:
time: 34.2 us; the launch traced here: 34.1 us
  Pallas kernels  32.5 us (95%)
  local copies, waits for them, and re-layouts  1.54 us (5%)
    pallas_call x1, Pallas kernels, dense(): pl.pallas_call(kernel, out_shape=jax.ShapeDtypeStruct(block, jnp.bfloat16...  32.5 us
    unnamed x1, local copies, waits for them, and re-layouts  1.54 us

profile of v3, /device:TPU:0, one launch (start us, length us, event | category | flops | bytes accessed | tf_op | source)
XLA Modules:
  0.0 34.1 jit_solution(16056228345215771441)
XLA Ops:
  0.0 32.5 %shard_map.64 = bf16[96,512]{1,0:T(8,128)(2,1)} custom-call(bf16[96,512]{1,0:T(8,128)(2,1)} %tokens.1, s32[2,96]{1,0:T(2,128)} %bitcast.3, bf16[4,2048]{1,0:T(4,128)(2,1)} %bitcast.2, bf16[1,2048,384]{2,1,0:T(8,128)(2,1)} %gate_w.1, bf16[1,2048,384]{2,1,0:T(8,128)(2,1)} %up_w.1, bf16[1,384,2048]{2,1,0:T(8,128)(2,1)} %down_w.1), custom_call_target="tpu_custom_call" | custom-call | tf_op jit(solution)/shard_map/pallas_call | solution.py:322
  32.5 1.5 %copy.8 = bf16[96,512]{1,0:T(8,128)(2,1)} copy(bf16[96,512]{1,0:T(8,128)(2,1)} %shard_map.64) | data formatting | bytes 196608

commit v4 on v3

--- a/solution.py
+++ b/solution.py
@@ -95,16 +95,15 @@
         loads.append(pltpu.make_async_copy(down_w.at[0, :, part], down.at[j], load_sem.at[9 + j]))
     loads.append(pltpu.make_async_copy(routes_hbm, routes, load_sem.at[13]))
     loads.append(pltpu.make_async_copy(router_hbm, router, load_sem.at[14]))
-    for load in loads:
-        load.start()
-
     barrier = pltpu.get_barrier_semaphore()
     partners = [(group, flip(sec, k), sub) for k in (1, 2, 3)]
-    partners += [(group, sec, flip(sub, j)) for j in (1, 2)]
+    partners = partners[::-1] + [(group, sec, flip(sub, j)) for j in (2, 1)]
     for partner in partners:
         pl.semaphore_signal(
             barrier, inc=1, device_id=partner, device_id_type=pl.DeviceIdType.MESH
         )
+    for load in loads:
+        load.start()
     pl.semaphore_wait(barrier, len(partners))
 
     used = [0]

time: 34.2 us -> 34.2 us (level)
  no operation moved by 1% of the time
where the time goes in v4:
time: 34.2 us; the launch traced here: 34.1 us
  Pallas kernels  32.5 us (95%)
  local copies, waits for them, and re-layouts  1.54 us (5%)
    pallas_call x1, Pallas kernels, dense(): pl.pallas_call(kernel, out_shape=jax.ShapeDtypeStruct(block, jnp.bfloat16...  32.5 us
    unnamed x1, local copies, waits for them, and re-layouts  1.54 us

profile of v4, /device:TPU:0, one launch (start us, length us, event | category | flops | bytes accessed | tf_op | source)
XLA Modules:
  0.0 34.1 jit_solution(711172099630197447)
XLA Ops:
  0.0 32.5 %shard_map.64 = bf16[96,512]{1,0:T(8,128)(2,1)} custom-call(bf16[96,512]{1,0:T(8,128)(2,1)} %tokens.1, s32[2,96]{1,0:T(2,128)} %bitcast.3, bf16[4,2048]{1,0:T(4,128)(2,1)} %bitcast.2, bf16[1,2048,384]{2,1,0:T(8,128)(2,1)} %gate_w.1, bf16[1,2048,384]{2,1,0:T(8,128)(2,1)} %up_w.1, bf16[1,384,2048]{2,1,0:T(8,128)(2,1)} %down_w.1), custom_call_target="tpu_custom_call" | custom-call | tf_op jit(solution)/shard_map/pallas_call | solution.py:321
  32.5 1.5 %copy.8 = bf16[96,512]{1,0:T(8,128)(2,1)} copy(bf16[96,512]{1,0:T(8,128)(2,1)} %shard_map.64) | data formatting | bytes 196608
